TPU v7x, 512 devices: a whole 4x4x16 slice. The times are simulated.
512 devices in a mesh: island: 4 (over x_hi, core), fsdp: 128 (over y, z, x_lo).
Axes of the slice: x: 4 (x_hi: 2, x_lo: 2; x = x_hi * 2 + x_lo), y: 4, z: 16, core: 2. Of those that a mesh axis runs over, the one named last changes fastest.
Arguments:
- tokens: bfloat16 [131072, 8192], P(('island', 'fsdp')), may hold values from -24 to 24
- key_grad: bfloat16 [131072, 128], P(('island', 'fsdp')), may hold values from -6 to 6
- weight: float32 [4, 8192, 128], P('island', 'fsdp'), may hold values from -6 to 6
- weight_m: float32 [4, 8192, 128], P('island', 'fsdp'), may hold values from -6 to 6
- weight_v: float32 [4, 8192, 128], P('island', 'fsdp'), may hold values from 0.1 to 10
- gain: float32 [4, 8192], P('island', 'fsdp'), may hold values from 0.1 to 1.9
- gain_m: float32 [4, 8192], P('island', 'fsdp'), may hold values from -24 to 24
- gain_v: float32 [4, 8192], P('island', 'fsdp'), may hold values from 10 to 1000
- outer: float32 [8192, 128], P('fsdp'), may hold values from -6 to 6
- momentum: float32 [8192, 128], P('fsdp'), may hold values from -3 to 3
- fragment_of_row: int32 [8192], P('fsdp'), may hold values from 0 to 3
- active_fragment: int32 [1], replicated, may hold values from 0 to 4095
Outputs:
- keys: bfloat16 [131072, 128], P(('island', 'fsdp'))
- new_weight: float32 [4, 8192, 128], P('island', 'fsdp')
- new_weight_m: float32 [4, 8192, 128], P('island', 'fsdp')
- new_weight_v: float32 [4, 8192, 128], P('island', 'fsdp')
- new_gain: float32 [4, 8192], P('island', 'fsdp')
- new_gain_m: float32 [4, 8192], P('island', 'fsdp')
- new_gain_v: float32 [4, 8192], P('island', 'fsdp')
- new_outer: float32 [8192, 128], P('fsdp')
- new_momentum: float32 [8192, 128], P('fsdp')
Inputs may be any that keep to these rules, and one draw needn't show every extreme that they name: `active_fragment`: an outer step number, zero or more.
All inputs are finite; a program needn't handle non-finite values.
Results may differ from a plain program's by a relative error of at most 0.009.
Values may be sent and summed in bfloat16 or wider, within the bound.
A program may use at most 128 MiB of HBM per device.

v0:
```python
import jax
import jax.numpy as jnp
from jax import lax
from jax.sharding import PartitionSpec as P

NFRAG = 4


NORM_EPS = 1e-05
BETA_ONE = 0.9
BETA_TWO = 0.999
ADAM_EPS = 1e-08
INNER_LR = 0.01
DECAY = 0.1
OUTER_LR = 0.7
OUTER_MU = 0.9
MIX_KEEP = 0.5


def adam_step(param, grad, first, second):
    first = BETA_ONE * first + (1.0 - BETA_ONE) * grad
    second = BETA_TWO * second + (1.0 - BETA_TWO) * grad * grad
    param = param - INNER_LR * (first / (jnp.sqrt(second) + ADAM_EPS) + DECAY * param)
    return (param, first, second)


def shards(
    tokens,
    key_grad,
    weight,
    weight_m,
    weight_v,
    gain,
    gain_m,
    gain_v,
    outer,
    momentum,
    fragment_of_row,
    active_fragment,
):
    model_width = tokens.shape[1]
    key_scale = model_width ** (-0.5)
    rows_here = weight.shape[1]
    outer_drift = lax.psum((outer - weight[0]).astype(jnp.bfloat16), "island").astype(
        jnp.float32
    ) / lax.axis_size("island")
    values = tokens.astype(jnp.float32)
    root_mean = jnp.sqrt(jnp.mean(values * values, axis=1) + NORM_EPS)
    unit_rows = values / root_mean[:, None]
    weight_bf = weight[0].astype(jnp.bfloat16)
    gain_bf = gain[0].astype(jnp.bfloat16)
    full_weight, full_gain = (
        lax.all_gather(weight_bf, "fsdp", axis=0, tiled=True),
        lax.all_gather(gain_bf, "fsdp", axis=0, tiled=True),
    )
    normed = (unit_rows * full_gain.astype(jnp.float32)).astype(jnp.bfloat16)
    key_total = jnp.dot(normed, full_weight, preferred_element_type=jnp.float32)
    back_grad = key_scale * jnp.dot(key_grad, full_weight.T, preferred_element_type=jnp.float32)
    gain_term = jnp.sum(back_grad * unit_rows, axis=0)
    keys = (key_scale * key_total).astype(jnp.bfloat16)
    weight_grad = lax.psum_scatter(
        key_scale
        * lax.dot_general(
            normed, key_grad, (((0,), (0,)), ((), ())), preferred_element_type=jnp.float32
        ),
        "fsdp",
        scatter_dimension=0,
        tiled=True,
    )
    gain_total = lax.psum(gain_term, "fsdp")
    gain_grad = lax.dynamic_slice_in_dim(
        gain_total, lax.axis_index("fsdp") * rows_here, rows_here, 0
    )
    inner, first, second = adam_step(weight[0], weight_grad, weight_m[0], weight_v[0])
    gain_new, gain_first, gain_second = adam_step(gain[0], gain_grad, gain_m[0], gain_v[0])
    pushed = OUTER_MU * momentum + outer_drift
    candidate = outer - OUTER_LR * (OUTER_MU * pushed + outer_drift)
    current = active_fragment[0] % NFRAG
    in_fragment = (fragment_of_row == current)[:, None]
    new_momentum = jnp.where(in_fragment, pushed, momentum)
    new_outer = jnp.where(in_fragment, candidate, outer)
    merged = jnp.where(in_fragment, MIX_KEEP * inner + (1.0 - MIX_KEEP) * candidate, inner)
    return (
        keys,
        merged[None],
        first[None],
        second[None],
        gain_new[None],
        gain_first[None],
        gain_second[None],
        new_outer,
        new_momentum,
    )


def solution(mesh):
    return jax.shard_map(
        shards,
        mesh=mesh,
        in_specs=(
            P(("island", "fsdp"), None),
            P(("island", "fsdp"), None),
            P("island", "fsdp", None),
            P("island", "fsdp", None),
            P("island", "fsdp", None),
            P("island", "fsdp"),
            P("island", "fsdp"),
            P("island", "fsdp"),
            P("fsdp", None),
            P("fsdp", None),
            P("fsdp"),
            P(),
        ),
        out_specs=(
            P(("island", "fsdp"), None),
            P("island", "fsdp", None),
            P("island", "fsdp", None),
            P("island", "fsdp", None),
            P("island", "fsdp"),
            P("island", "fsdp"),
            P("island", "fsdp"),
            P("fsdp", None),
            P("fsdp", None),
        ),
        check_vma=False,
    )
```

profile of v0, /device:TPU:6, one launch (start us, length us, event | category | flops | bytes accessed | tf_op | source)
XLA Modules:
  0.0 1272.0 jit_solution(18086172306200970475)
XLA Ops:
  7.2 0.0 copy-start
  7.2 0.0 all-gather.2.cloned.1.call-start
  7.2 1.4 bitcast_convert_fusion
  8.6 0.0 all-gather.2.cloned.1.call-update
  8.6 0.0 reduce-scatter.2.cloned.1.call-start
  8.7 1.3 dynamic-slice
  10.6 0.7 bitcast_convert_fusion.1
  11.3 0.2 dynamic-update-slice
  11.5 611.4 %all-reduce = bf16[8192]{0:T(1024)(128)(2,1)S(1)} all-reduce(bf16[8192]{0:T(1024)(128)(2,1)S(1)} %dynamic-update-slice), channel_id=1, replica_groups=mesh['island'=4,'fsdp'=128] {'fsdp'}, use_global_device_ids=true, to_apply=%add | all-reduce | flops 8192 | bytes 32768
  622.9 3.3 fusion.1
  626.1 0.2 copy-done.2
  626.3 1.2 multiply_convert_fusion
  627.6 1.9 copy-done.1
  629.5 3.3 convolution_multiply_fusion.1
  632.8 0.0 reduce-scatter.2.cloned.1.call-update
  633.5 0.0 copy-done.4
  633.5 0.0 copy-done.5
  633.6 13.1 %psum.14 = bf16[64,128]{1,0:T(8,128)(2,1)S(1)} all-reduce(bf16[64,128]{1,0:T(8,128)(2,1)S(1)} %fusion.7), channel_id=1, replica_groups=mesh['island'=4,'fsdp'=128] {'island'}, use_global_device_ids=true, to_apply=%region_2.0 | all-reduce | flops 8192 | bytes 32768 | tf_op jit(solution)/shard_map/psum | solution.py:44
  646.7 0.0 all-gather.2.cloned.1.call-done
  646.8 4.7 fusion.2
  651.6 607.4 %psum.15 = f32[8192]{0:T(1024)S(1)} all-reduce(f32[8192]{0:T(1024)S(1)} %fusion.2), channel_id=1, replica_groups=mesh['island'=4,'fsdp'=128] {'fsdp'}, use_global_device_ids=true, to_apply=%region_4.0 | all-reduce | flops 8192 | bytes 65536 | tf_op jit(solution)/shard_map/psum | solution.py:70
  1259.0 0.6 fusion.15
  1259.6 4.1 fusion.3
  1263.7 1.5 broadcast_select_fusion
  (27 shorter events, 0.1 us)
Async XLA Ops:
  7.2 622.3 %copy-start = (bf16[256,128]{1,0:T(8,128)(2,1)S(1)}, bf16[256,128]{1,0:T(8,128)(2,1)}, u32[]{:S(2)}) copy-start(bf16[256,128]{1,0:T(8,128)(2,1)} %param.13) | copy-start | bytes 196612
  7.2 639.6 %all-gather.2.cloned.1.call-start = ((), (), s32[]{:S(2)}) async-start(), calls=%async_computation.1 | async-start | bytes 2113536 | tf_op jit(solution)/shard_map/all_gather | solution.py:53
  8.6 1255.0 %reduce-scatter.2.cloned.1.call-start = ((), (), s32[]{:S(2)}) async-start(), calls=%async_computation.2 | async-start | bytes 4227072 | tf_op jit(solution)/shard_map/reduce_scatter | solution.py:61
  622.9 3.4 copy-start.2
  627.5 1.9 copy-start.1
  632.8 0.8 copy-start.4
  632.8 0.8 copy-start.5
  632.8 13.9 %copy-start.12 = (s32[64]{0:T(128)S(1)}, s32[64]{0:T(128)}, u32[]{:S(2)}) copy-start(s32[64]{0:T(128)} %param.22) | copy-start | bytes 772
  646.7 612.3 %copy-start.9 = (f32[1,64]{1,0:T(1,128)S(1)}, f32[1,64]{1,0:T(1,128)}, u32[]{:S(2)}) copy-start(f32[1,64]{1,0:T(1,128)} %param.17) | copy-start | bytes 772
  646.7 612.3 %copy-start.10 = (f32[1,64]{1,0:T(1,128)S(1)}, f32[1,64]{1,0:T(1,128)}, u32[]{:S(2)}) copy-start(f32[1,64]{1,0:T(1,128)} %param.19) | copy-start | bytes 772
  646.7 612.3 %copy-start.11 = (f32[1,64]{1,0:T(1,128)S(1)}, f32[1,64]{1,0:T(1,128)}, u32[]{:S(2)}) copy-start(f32[1,64]{1,0:T(1,128)} %param.18) | copy-start | bytes 772
  646.8 612.8 %copy-start.3 = (bf16[8192,128]{1,0:T(8,128)(2,1)S(1)}, bf16[8192,128]{1,0:T(8,128)(2,1)}, u32[]{:S(2)}) copy-start(bf16[8192,128]{1,0:T(8,128)(2,1)} %all-gather.2.cloned.1.call-done) | copy-start | bytes 6291460
  651.5 612.1 %copy-start.6 = (f32[64,128]{1,0:T(8,128)S(1)}, f32[64,128]{1,0:T(8,128)}, u32[]{:S(2)}) copy-start(f32[64,128]{1,0:T(8,128)} %param.21) | copy-start | bytes 98308
  651.5 612.1 %copy-start.7 = (f32[1,64,128]{2,1,0:T(8,128)S(1)}, f32[1,64,128]{2,1,0:T(8,128)}, u32[]{:S(2)}) copy-start(f32[1,64,128]{2,1,0:T(8,128)} %param.16) | copy-start | bytes 98308
  651.5 612.1 %copy-start.8 = (f32[1,64,128]{2,1,0:T(8,128)S(1)}, f32[1,64,128]{2,1,0:T(8,128)}, u32[]{:S(2)}) copy-start(f32[1,64,128]{2,1,0:T(8,128)} %param.15) | copy-start | bytes 98308
Sparse Core Ops, SparseCore 0:
  10.7 592.4 all-gather.1
  632.9 620.8 reduce-scatter.1
where the time goes:
time: 1280 us; the launch traced here: 1270 us
  blocking collectives  1230 us (96%)
  between operations  15.5 us (1%)
    unnamed x1, blocking collectives  611 us
    psum x1, blocking collectives, shards(): gain_total = lax.psum(gain_term, 'fsdp')  607 us
  transfers between devices with their start and end apart: 2, of which 0 were waited for; matrix products, arithmetic and copies ran while one was open for 2% of the time, Pallas kernels for 0%

commit v1 on v0

v1 whole, which is shorter than its diff:
```python
import jax
import jax.numpy as jnp
from jax import lax
from jax.experimental import pallas as pl
from jax.experimental.pallas import tpu as pltpu
from jax.sharding import PartitionSpec as P

NFRAG = 4
NORM_EPS = 1e-05
BETA_ONE = 0.9
BETA_TWO = 0.999
ADAM_EPS = 1e-08
INNER_LR = 0.01
DECAY = 0.1
OUTER_LR = 0.7
OUTER_MU = 0.9
MIX_KEEP = 0.5

MESH = pl.DeviceIdType.MESH
NY, NZ, NX, NI = 4, 16, 2, 4
TOK, WIDTH, HEAD = 256, 8192, 128
ROWS = 64
BLOCK = NX * ROWS
YSTEP = (0, 1, 3, 2)
F32, BF16 = jnp.float32, jnp.bfloat16


def exchange(
    x_hbm,
    kg,
    weight,
    gain,
    outer,
    keys_out,
    usum_out,
    drift_out,
    xv,
    gw,
    part,
    s_a,
    r_a,
    s_bp,
    s_bm,
    r_bp,
    r_bm,
    s_zp,
    s_zm,
    r_zp,
    r_zm,
    own,
    total,
    r_x,
    diffs,
    acc,
    kgt,
    inv,
    sem_x,
    gz_recv,
    gx_recv,
    gy_recv,
    g_send,
    a_recv,
    b_recv,
    z_recv,
    rs_send,
    tail_send,
    tail_recv,
    d_send,
    d_recv,
):
    isl, f = lax.axis_index("island"), lax.axis_index("fsdp")
    y, z, xl = f // (NZ * NX), (f // NX) % NZ, f % NX

    def device(dy=0, dz=0, flip=False):
        yy, zz = (y + NY + dy) % NY, (z + NZ + dz) % NZ
        xx = 1 - xl if flip else xl
        return (isl, (yy * NZ + zz) * NX + xx)

    up_y, down_y, up_z, down_z = device(dy=1), device(dy=-1), device(dz=1), device(dz=-1)
    partner = device(flip=True)
    islands = [((isl + k) % NI, f) for k in range(1, NI)]

    barrier = pltpu.get_barrier_semaphore()
    peers = [up_y, down_y, up_z, down_z, partner] + islands
    for peer in peers:
        pl.semaphore_signal(barrier, inc=1, device_id=peer, device_id_type=MESH)

    def load(n, carry):
        for c in range(2):
            r = 8 - n if c == 0 else (8 + n + 8 * ((8 - n) // 8)) % NZ
            for p in range(NY):
                block = ((y + YSTEP[p]) % NY) * NZ + (z + r) % NZ
                pltpu.make_async_copy(
                    x_hbm.at[:, pl.ds(pl.multiple_of(block * BLOCK, BLOCK), BLOCK)],
                    xv.at[n, :, pl.ds((c * NY + p) * BLOCK, BLOCK)],
                    sem_x.at[n],
                ).start()
        return carry

    lax.fori_loop(0, 8, load, 0)

    def remote(src, dst, send, recv, to):
        return pltpu.make_async_remote_copy(
            src_ref=src,
            dst_ref=dst,
            send_sem=send,
            recv_sem=recv,
            device_id=to,
            device_id_type=MESH,
        )

    def await_recv(ref, sem):
        pltpu.make_async_copy(ref, ref, sem).wait()

    half = pl.ds(pl.multiple_of(xl * ROWS, ROWS), ROWS)
    other = pl.ds(pl.multiple_of((1 - xl) * ROWS, ROWS), ROWS)
    low = pl.ds(pl.multiple_of(xl * ROWS, ROWS), ROWS // 2)
    high = pl.ds(pl.multiple_of(xl * ROWS + ROWS // 2, ROWS // 2), ROWS // 2)

    eye = lax.broadcasted_iota(jnp.int32, (ROWS, ROWS), 0) == lax.broadcasted_iota(
        jnp.int32, (ROWS, ROWS), 1
    )
    gain_bf = gain[...].astype(BF16).astype(F32)
    column = jnp.sum(jnp.where(eye, gain_bf, 0.0), axis=1, keepdims=True)
    w = weight[0]
    gw[1, 0, half, :] = (column * w.astype(BF16).astype(F32)).astype(BF16)
    diffs[isl] = (outer[...] - w).astype(BF16)

    pl.semaphore_wait(barrier, len(peers))

    mine = gw.at[1, 0, half]
    remote(mine, mine, g_send.at[0], gx_recv.at[16], partner).start()
    remote(mine, gw.at[1, 2, half], g_send.at[1], gy_recv.at[2], up_y).start()
    remote(mine, gw.at[1, 1, half], g_send.at[2], gy_recv.at[1], down_y).start()
    for k in range(1, NI):
        remote(
            diffs.at[isl], diffs.at[isl], d_send.at[k], d_recv.at[NI - k], islands[k - 1]
        ).start()

    def rows(p):
        return pl.ds(0, BLOCK) if p == 0 else half

    def send_z(p, c, src, dst):
        to = down_z if c == 0 else up_z
        remote(
            gw.at[src, p, rows(p)],
            gw.at[dst, p, rows(p)],
            g_send.at[3 if p == 0 else 4],
            gz_recv.at[dst, p],
            to,
        ).start()

    def wait_z(p, n, c):
        await_recv(gw.at[2 * n + c, p, rows(p)], gz_recv.at[2 * n + c, p])

    def send_x(n, c):
        block = gw.at[2 * n + c, pl.ds(1, 3), half]
        remote(block, block, g_send.at[5], gx_recv.at[2 * n + c], partner).start()

    def wait_x(n, c):
        await_recv(gw.at[2 * n + c, pl.ds(1, 3), other], gx_recv.at[2 * n + c])

    def squares(n, carry):
        await_recv(xv.at[n], sem_x.at[n])
        for k in range(2 * NY):
            v = xv[n, :, k * BLOCK : (k + 1) * BLOCK].astype(F32)
            inv[...] += v * v
        return carry

    inv[...] = jnp.zeros_like(inv)
    acc[...] = jnp.zeros_like(acc)
    lax.fori_loop(0, 4, squares, 0)
    await_recv(gw.at[1, 0, other], gx_recv.at[16])
    for c in range(2):
        send_z(0, c, 1, 14 + c)
    await_recv(gw.at[1, 2, half], gy_recv.at[2])
    remote(gw.at[1, 2, low], gw.at[1, 3, low], g_send.at[6], gy_recv.at[3], up_y).start()
    await_recv(gw.at[1, 1, half], gy_recv.at[1])
    remote(gw.at[1, 1, high], gw.at[1, 3, high], g_send.at[7], gy_recv.at[4], down_y).start()
    for p in (1, 2):
        for c in range(2):
            send_z(p, c, 1, 14 + c)
    lax.fori_loop(4, 8, squares, 0)
    scale = lax.rsqrt(jnp.sum(inv[...], axis=1, keepdims=True) * (1.0 / WIDTH) + NORM_EPS)
    inv[...] = jnp.broadcast_to(scale, inv.shape)
    kgt[...] = (kg[...].astype(F32) * inv[...]).T.astype(BF16)

    def block_of(n, c, p):
        lanes = (c * NY + p) * BLOCK
        return part[n, :, lanes : lanes + BLOCK]

    def step_one(n):
        part[n] = jnp.dot(kgt[...], xv[n], preferred_element_type=F32)
        for c in range(2):
            s_a[n, c] = block_of(n, c, 3).astype(BF16)
        top, bottom = pl.ds(0, HEAD // 2), pl.ds(HEAD // 2, HEAD // 2)
        remote(
            s_a.at[n, :, top], r_a.at[n, :, top], rs_send.at[0], a_recv.at[n, 0], up_y
        ).start()
        remote(
            s_a.at[n, :, bottom], r_a.at[n, :, bottom], rs_send.at[0], a_recv.at[n, 1], down_y
        ).start()

    def step_two(n):
        h = HEAD // 2
        await_recv(r_a.at[n, :, pl.ds(0, h)], a_recv.at[n, 0])
        for c in range(2):
            mine = block_of(n, c, 1)
            s_bp[n, c, :h] = (mine[:h] + r_a[n, c, :h].astype(F32)).astype(BF16)
            s_bp[n, c, h:] = mine[h:].astype(BF16)
        remote(s_bp.at[n], r_bp.at[n], rs_send.at[1], b_recv.at[n, 0], up_y).start()
        await_recv(r_a.at[n, :, pl.ds(h, h)], a_recv.at[n, 1])
        for c in range(2):
            mine = block_of(n, c, 2)
            s_bm[n, c, :h] = mine[:h].astype(BF16)
            s_bm[n, c, h:] = (mine[h:] + r_a[n, c, h:].astype(F32)).astype(BF16)
        remote(s_bm.at[n], r_bm.at[n], rs_send.at[2], b_recv.at[n, 1], down_y).start()

    r_zp[0] = jnp.zeros((HEAD, BLOCK), BF16)
    r_zm[0] = jnp.zeros((HEAD, BLOCK), BF16)
    r_zm[1] = jnp.zeros((HEAD, BLOCK), BF16)

    def step_three(n):
        await_recv(r_bp.at[n], b_recv.at[n, 0])
        await_recv(r_bm.at[n], b_recv.at[n, 1])
        sums = [
            block_of(n, c, 0) + r_bp[n, c].astype(F32) + r_bm[n, c].astype(F32) for c in range(2)
        ]

        @pl.when(n >= 1)
        def _():
            await_recv(r_zp.at[n], z_recv.at[n, 0])

        s_zp[n] = (sums[0] + r_zp[n].astype(F32)).astype(BF16)
        remote(s_zp.at[n], r_zp.at[n + 1], rs_send.at[3], z_recv.at[n + 1, 0], up_z).start()

        @pl.when(n == 0)
        def _():
            own[...] = sums[1]

        @pl.when(n >= 2)
        def _():
            await_recv(r_zm.at[n], z_recv.at[n, 1])

        @pl.when(n >= 1)
        def _():
            s_zm[n] = (sums[1] + r_zm[n].astype(F32)).astype(BF16)
            remote(
                s_zm.at[n], r_zm.at[n + 1], rs_send.at[4], z_recv.at[n + 1, 1], down_z
            ).start()

    def keys_part(n):
        for c in range(2):
            wait_x(n, c)
        acc[...] += jnp.dot(
            xv[n], gw[pl.ds(2 * n, 2)].reshape(2 * NY * BLOCK, HEAD), preferred_element_type=F32
        )

    step_one(0)
    await_recv(gw.at[1, 3, low], gy_recv.at[3])
    await_recv(gw.at[1, 3, high], gy_recv.at[4])
    for c in range(2):
        send_z(3, c, 1, 14 + c)
    send_x(0, 1)

    def iteration(i, carry):
        @pl.when(i <= 6)
        def _():
            n = 8 - i
            for p in range(NY):
                for c in range(2):
                    wait_z(p, n, c)
                    send_z(p, c, 2 * n + c, 2 * n - 2 + c)
            for c in range(2):
                send_x(n, c)

        @pl.when(i == 7)
        def _():
            for p in range(NY):
                for c in range(2):
                    wait_z(p, 1, c)
                    if c == (1 if p < 2 else 0):
                        send_z(p, c, 2 + c, 0)
            for c in range(2):
                send_x(1, c)

        @pl.when(i == 8)
        def _():
            for p in range(NY):
                wait_z(p, 0, 0)
            send_x(0, 0)

        @pl.when(i <= 7)
        def _():
            step_one(i)

        @pl.when(i <= 8)
        def _():
            step_two(i - 1)

        @pl.when(i >= 2)
        def _():
            step_three(i - 2)
            keys_part(9 - i)

        return carry

    lax.fori_loop(1, 10, iteration, 0)

    await_recv(r_zp.at[8], z_recv.at[8, 0])
    await_recv(r_zm.at[8], z_recv.at[8, 1])
    total[...] = (own[...] + r_zp[8].astype(F32) + r_zm[8].astype(F32)).T
    remote(total.at[other], r_x, tail_send, tail_recv, partner).start()

    keys_out[...] = (acc[...] * (inv[...] * WIDTH ** (-0.5))).astype(BF16)
    for k in range(1, NI):
        await_recv(diffs.at[(isl + k) % NI], d_recv.at[k])
    summed = diffs[0].astype(F32)
    for k in range(1, NI):
        summed = summed + diffs[k].astype(F32)
    drift_out[...] = summed * (1.0 / NI)

    for k in (0, 1, 2):
        await_recv(mine, g_send.at[k])
    await_recv(gw.at[pl.ds(1, 15), 0], g_send.at[3])
    await_recv(gw.at[pl.ds(1, 15), pl.ds(1, 3), half], g_send.at[4])
    await_recv(gw.at[:, pl.ds(1, 3), half], g_send.at[5])
    await_recv(gw.at[1, 3, low], g_send.at[6])
    await_recv(gw.at[1, 3, high], g_send.at[7])
    for k in range(1, NI):
        await_recv(diffs.at[0], d_send.at[k])
    await_recv(s_a, rs_send.at[0])
    await_recv(s_bp, rs_send.at[1])
    await_recv(s_bm, rs_send.at[2])
    await_recv(s_zp, rs_send.at[3])
    await_recv(s_zm.at[pl.ds(1, 7)], rs_send.at[4])
    await_recv(total.at[other], tail_send)

    await_recv(r_x, tail_recv)
    usum_out[...] = total[half, :] + r_x[...]


def adam_step(param, grad, first, second):
    first = BETA_ONE * first + (1.0 - BETA_ONE) * grad
    second = BETA_TWO * second + (1.0 - BETA_TWO) * grad * grad
    param = param - INNER_LR * (first / (jnp.sqrt(second) + ADAM_EPS) + DECAY * param)
    return (param, first, second)


def shards(
    tokens,
    key_grad,
    weight,
    weight_m,
    weight_v,
    gain,
    gain_m,
    gain_v,
    outer,
    momentum,
    fragment_of_row,
    active_fragment,
):
    vmem = pl.BlockSpec(memory_space=pltpu.VMEM)
    block = (HEAD, BLOCK)
    dma = pltpu.SemaphoreType.DMA
    keys, unit_sum, outer_drift = pl.pallas_call(
        exchange,
        out_shape=(
            jax.ShapeDtypeStruct((TOK, HEAD), BF16),
            jax.ShapeDtypeStruct((ROWS, HEAD), F32),
            jax.ShapeDtypeStruct((ROWS, HEAD), F32),
        ),
        in_specs=[pl.BlockSpec(memory_space=pl.ANY)] + [vmem] * 4,
        out_specs=(vmem, vmem, vmem),
        scratch_shapes=[
            pltpu.VMEM((8, TOK, 2 * NY * BLOCK), BF16),
            pltpu.VMEM((NZ, NY, BLOCK, HEAD), BF16),
            pltpu.VMEM((8, HEAD, 2 * NY * BLOCK), F32),
            pltpu.VMEM((8, 2) + block, BF16),
            pltpu.VMEM((8, 2) + block, BF16),
            pltpu.VMEM((8, 2) + block, BF16),
            pltpu.VMEM((8, 2) + block, BF16),
            pltpu.VMEM((8, 2) + block, BF16),
            pltpu.VMEM((8, 2) + block, BF16),
            pltpu.VMEM((8,) + block, BF16),
            pltpu.VMEM((8,) + block, BF16),
            pltpu.VMEM((9,) + block, BF16),
            pltpu.VMEM((9,) + block, BF16),
            pltpu.VMEM(block, F32),
            pltpu.VMEM(block, F32),
            pltpu.VMEM((ROWS, HEAD), F32),
            pltpu.VMEM((NI, ROWS, HEAD), BF16),
            pltpu.VMEM((TOK, HEAD), F32),
            pltpu.VMEM((HEAD, TOK), BF16),
            pltpu.VMEM((TOK, HEAD), F32),
            dma((8,)),
            dma((NZ, NY)),
            dma((NZ + 1,)),
            dma((5,)),
            dma((8,)),
            dma((8, 2)),
            dma((8, 2)),
            dma((9, 2)),
            dma((5,)),
            dma,
            dma,
            dma((NI,)),
            dma((NI,)),
        ],
        compiler_params=pltpu.CompilerParams(
            collective_id=0, has_side_effects=True, vmem_limit_bytes=40 * 2**20
        ),
        cost_estimate=pl.CostEstimate(
            flops=4 * TOK * WIDTH * HEAD, bytes_accessed=2 * TOK * WIDTH, transcendentals=0
        ),
    )(tokens, key_grad, weight, gain, outer)
    key_scale = WIDTH ** (-0.5)
    weight_bf = weight[0].astype(BF16).astype(F32)
    gain_bf = gain[0].astype(BF16).astype(F32)
    weight_grad = key_scale * gain_bf[:, None] * unit_sum
    gain_grad = key_scale * jnp.sum(weight_bf * unit_sum, axis=1)
    inner, first, second = adam_step(weight[0], weight_grad, weight_m[0], weight_v[0])
    gain_new, gain_first, gain_second = adam_step(gain[0], gain_grad, gain_m[0], gain_v[0])
    pushed = OUTER_MU * momentum + outer_drift
    candidate = outer - OUTER_LR * (OUTER_MU * pushed + outer_drift)
    current = active_fragment[0] % NFRAG
    in_fragment = (fragment_of_row == current)[:, None]
    new_momentum = jnp.where(in_fragment, pushed, momentum)
    new_outer = jnp.where(in_fragment, candidate, outer)
    merged = jnp.where(in_fragment, MIX_KEEP * inner + (1.0 - MIX_KEEP) * candidate, inner)
    return (
        keys,
        merged[None],
        first[None],
        second[None],
        gain_new[None],
        gain_first[None],
        gain_second[None],
        new_outer,
        new_momentum,
    )


def solution(mesh):
    return jax.shard_map(
        shards,
        mesh=mesh,
        in_specs=(
            P(("island", "fsdp"), None),
            P(("island", "fsdp"), None),
            P("island", "fsdp", None),
            P("island", "fsdp", None),
            P("island", "fsdp", None),
            P("island", "fsdp"),
            P("island", "fsdp"),
            P("island", "fsdp"),
            P("fsdp", None),
            P("fsdp", None),
            P("fsdp"),
            P(),
        ),
        out_specs=(
            P(("island", "fsdp"), None),
            P("island", "fsdp", None),
            P("island", "fsdp", None),
            P("island", "fsdp", None),
            P("island", "fsdp"),
            P("island", "fsdp"),
            P("island", "fsdp"),
            P("fsdp", None),
            P("fsdp", None),
        ),
        check_vma=False,
    )
```

time: 1280 us -> 69.1 us (0.05)
  the two profiles are of different devices: /device:TPU:6 before, /device:TPU:2 now
where the time goes in v1:
time: 69.1 us; the launch traced here: 68.6 us
  Pallas kernels  58.7 us (85%)
  local copies, waits for them, and re-layouts  5.84 us (8%)
  other arithmetic  2.7 us (4%)
  between operations  1.38 us (2%)
    pallas_call x1, Pallas kernels, shards(): pl.pallas_call(exchange, out_shape=(jax.ShapeDtypeStruct((TOK, HEAD), BF1...  58.7 us
    unnamed x21, local copies, waits for them, and re-layouts  5.84 us

profile of v1, /device:TPU:2, one launch (start us, length us, event | category | flops | bytes accessed | tf_op | source)
XLA Modules:
  0.0 68.6 jit_solution(9158214413757072815)
XLA Ops:
  0.6 0.0 copy-start.5
  1.3 0.7 broadcast_compare_fusion
  2.0 0.7 multiply_bitcast_fusion
  2.6 0.0 copy-start
  2.6 2.2 %copy-done = bf16[256,8192]{1,0:T(8,128)(2,1)S(1)} copy-done((bf16[256,8192]{1,0:T(8,128)(2,1)S(1)}, bf16[256,8192]{1,0:T(8,128)(2,1)}, u32[]{:S(2)}) %copy-start) | copy-done | bytes 4194328
  4.8 0.0 copy-start.1
  4.8 0.8 %copy-done.1 = f32[1,64,128]{2,1,0:T(8,128)S(1)} copy-done((f32[1,64,128]{2,1,0:T(8,128)S(1)}, f32[1,64,128]{2,1,0:T(8,128)}, u32[]{:S(2)}) %copy-start.1) | copy-done | bytes 32792
  5.6 0.0 copy-start.2
  5.6 0.8 %copy-done.2 = f32[64,128]{1,0:T(8,128)S(1)} copy-done((f32[64,128]{1,0:T(8,128)S(1)}, f32[64,128]{1,0:T(8,128)}, u32[]{:S(2)}) %copy-start.2) | copy-done | bytes 32792
  6.3 0.0 copy-start.3
  6.3 0.8 %copy-done.3 = bf16[256,128]{1,0:T(8,128)(2,1)S(1)} copy-done((bf16[256,128]{1,0:T(8,128)(2,1)S(1)}, bf16[256,128]{1,0:T(8,128)(2,1)}, u32[]{:S(2)}) %copy-start.3) | copy-done | bytes 65560
  7.2 0.0 copy-start.4
  7.2 0.7 copy-done.4
  7.8 0.0 copy-start.6
  7.8 0.0 copy-start.7
  7.9 58.7 %shard_map.187 = (bf16[256,128]{1,0:T(8,128)(2,1)S(1)}, f32[64,128]{1,0:T(8,128)S(1)}, f32[64,128]{1,0:T(8,128)S(1)}) custom-call(bf16[256,8192]{1,0:T(8,128)(2,1)S(1)} %copy-done, bf16[256,128]{1,0:T(8,128)(2,1)S(1)} %copy-done.3, f32[1,64,128]{2,1,0:T(8,128)S(1)} %copy-done.1, f32[1,64]{1,0:T(1,128)S(1)} %copy-done.4, f32[64,128]{1,0:T(8,128)S(1)} %copy-done.2), custom_call_target="tpu_custom_call" | custom-call | flops 1073741824 | bytes 4194304 | tf_op jit(solution)/shard_map/pallas_call | solution.py:367
  66.5 0.0 copy-done.5
  66.5 0.0 copy-done.6
  66.5 0.0 copy-done.7
  66.6 0.8 %broadcast_select_fusion = (f32[64,128]{1,0:T(8,128)}, f32[1,64,128]{2,1,0:T(8,128)}, f32[1,64,128]{2,1,0:T(8,128)}, f32[1,64,128]{2,1,0:T(8,128)}, f32[64,128]{1,0:T(8,128)}, /*index=5*/f32[64]{0:T(128)S(1)}) fusion(f32[64,128]{1,0:T(8,128)S(1)} %copy-done.2, pred[64]{0:T(512)(128)(4,1)S(1)} %broadcast_compare_fusion, f32[64,128]{1,0:T(8,128)S(1)} %get-tuple-element.14, ...), kind=kLoop, calls=%fused_computation.13 | loop fusion | flops 237504 | bytes 393792 | tf_op jit(solution)/shard_map/jit(_where)/select_n | solution.py:430
  67.4 0.0 copy-done.8
  67.4 0.0 copy-done.9
  67.4 0.5 multiply_subtract_fusion.1
  68.0 0.6 copy.23
  (2 shorter events, 0.0 us)
Async XLA Ops:
  0.6 65.9 %copy-start.5 = (f32[64,128]{1,0:T(8,128)S(1)}, f32[64,128]{1,0:T(8,128)}, u32[]{:S(2)}) copy-start(f32[64,128]{1,0:T(8,128)} %param.21) | copy-start | bytes 98308
  2.6 2.2 %copy-start = (bf16[256,8192]{1,0:T(8,128)(2,1)S(1)}, bf16[256,8192]{1,0:T(8,128)(2,1)}, u32[]{:S(2)}) copy-start(bf16[256,8192]{1,0:T(8,128)(2,1)} %x_hbm.1) | copy-start | bytes 12582916
  4.8 0.8 %copy-start.1 = (f32[1,64,128]{2,1,0:T(8,128)S(1)}, f32[1,64,128]{2,1,0:T(8,128)}, u32[]{:S(2)}) copy-start(f32[1,64,128]{2,1,0:T(8,128)} %weight.1) | copy-start | bytes 98308
  5.6 0.8 %copy-start.2 = (f32[64,128]{1,0:T(8,128)S(1)}, f32[64,128]{1,0:T(8,128)}, u32[]{:S(2)}) copy-start(f32[64,128]{1,0:T(8,128)} %outer.1) | copy-start | bytes 98308
  6.3 0.8 %copy-start.3 = (bf16[256,128]{1,0:T(8,128)(2,1)S(1)}, bf16[256,128]{1,0:T(8,128)(2,1)}, u32[]{:S(2)}) copy-start(bf16[256,128]{1,0:T(8,128)(2,1)} %kg.1) | copy-start | bytes 196612
  7.2 0.7 copy-start.4
  7.8 58.7 %copy-start.6 = (f32[1,64,128]{2,1,0:T(8,128)S(1)}, f32[1,64,128]{2,1,0:T(8,128)}, u32[]{:S(2)}) copy-start(f32[1,64,128]{2,1,0:T(8,128)} %param.16) | copy-start | bytes 98308
  7.8 58.7 %copy-start.7 = (f32[1,64,128]{2,1,0:T(8,128)S(1)}, f32[1,64,128]{2,1,0:T(8,128)}, u32[]{:S(2)}) copy-start(f32[1,64,128]{2,1,0:T(8,128)} %param.15) | copy-start | bytes 98308
  7.8 59.6 %copy-start.8 = (f32[1,64]{1,0:T(1,128)S(1)}, f32[1,64]{1,0:T(1,128)}, u32[]{:S(2)}) copy-start(f32[1,64]{1,0:T(1,128)} %param.19) | copy-start | bytes 772
  7.8 59.6 %copy-start.9 = (f32[1,64]{1,0:T(1,128)S(1)}, f32[1,64]{1,0:T(1,128)}, u32[]{:S(2)}) copy-start(f32[1,64]{1,0:T(1,128)} %param.18) | copy-start | bytes 772

commit v2 on v0

v2 whole, which is shorter than its diff:
```python
import jax
import jax.numpy as jnp
from jax import lax
from jax.experimental import pallas as pl
from jax.experimental.pallas import tpu as pltpu
from jax.sharding import PartitionSpec as P

NFRAG = 4
NORM_EPS = 1e-05
BETA_ONE = 0.9
BETA_TWO = 0.999
ADAM_EPS = 1e-08
INNER_LR = 0.01
DECAY = 0.1
OUTER_LR = 0.7
OUTER_MU = 0.9
MIX_KEEP = 0.5

MESH = pl.DeviceIdType.MESH
NY, NZ, NX, NI = 4, 16, 2, 4
TOK, WIDTH, HEAD = 256, 8192, 128
ROWS = 64
BLOCK = NX * ROWS
ZSTEP = (0, 1, -2, -1)
ORDER = (2, 1, 3, 0)
GROUP = NY * 4 * BLOCK
F32, BF16 = jnp.float32, jnp.bfloat16


def exchange(
    x_hbm,
    kg_hbm,
    weight_hbm,
    gain_hbm,
    outer_hbm,
    keys_out,
    usum_out,
    drift_out,
    xv,
    gw,
    part,
    s_a,
    r_a,
    s_bp,
    s_bm,
    r_bp,
    r_bm,
    s_z,
    r_z,
    s_h,
    r_h,
    own,
    total,
    r_x,
    diffs,
    acc,
    kgt,
    inv,
    kg,
    weight,
    gain,
    outer,
    sem_in,
    sem_x,
    gh_recv,
    gz_recv,
    gy_recv,
    gx_recv,
    g_send,
    a_recv,
    b_recv,
    z_recv,
    h_recv,
    rs_send,
    tail_send,
    tail_recv,
    d_send,
    d_recv,
):
    isl, f = lax.axis_index("island"), lax.axis_index("fsdp")
    y, z, xl = f // (NZ * NX), (f // NX) % NZ, f % NX

    def device(dy=0, dz=0, flip=False):
        yy, zz = (y + NY + dy) % NY, (z + NZ + dz) % NZ
        xx = 1 - xl if flip else xl
        return (isl, (yy * NZ + zz) * NX + xx)

    loads = [
        pltpu.make_async_copy(src, dst, sem_in.at[k])
        for k, (src, dst) in enumerate(
            [(weight_hbm, weight), (gain_hbm, gain), (outer_hbm, outer), (kg_hbm, kg)]
        )
    ]
    for copy in loads:
        copy.start()
    up_y, down_y = device(dy=1), device(dy=-1)
    near = {d: device(dz=d) for d in (1, -1, 2, -2)}
    far = {k: device(dz=d) for k, d in ((1, 4), (2, 8), (3, -4))}
    partner = device(flip=True)
    islands = [((isl + k) % NI, f) for k in range(1, NI)]

    barrier = pltpu.get_barrier_semaphore()
    peers = [up_y, down_y, partner] + list(near.values()) + list(far.values()) + islands
    for peer in peers:
        pl.semaphore_signal(barrier, inc=1, device_id=peer, device_id_type=MESH)

    def load(k):
        def one(q, carry):
            for j in range(4):
                block = ((y + q) % NY) * NZ + (z + NZ + 4 * k + ZSTEP[j]) % NZ
                pltpu.make_async_copy(
                    x_hbm.at[:, pl.ds(pl.multiple_of(block * BLOCK, BLOCK), BLOCK)],
                    xv.at[k, :, pl.ds(pl.multiple_of((q * 4 + j) * BLOCK, BLOCK), BLOCK)],
                    sem_x.at[k],
                ).start()
            return carry

        lax.fori_loop(0, NY, one, 0)

    for k in ORDER:
        load(k)

    def remote(src, dst, send, recv, to):
        return pltpu.make_async_remote_copy(
            src_ref=src,
            dst_ref=dst,
            send_sem=send,
            recv_sem=recv,
            device_id=to,
            device_id_type=MESH,
        )

    def await_recv(ref, sem):
        pltpu.make_async_copy(ref, ref, sem).wait()

    half = pl.ds(pl.multiple_of(xl * ROWS, ROWS), ROWS)
    other = pl.ds(pl.multiple_of((1 - xl) * ROWS, ROWS), ROWS)
    first, last = pl.ds(0, 2), pl.ds(2, 2)

    for copy in loads[:3]:
        copy.wait()
    eye = lax.broadcasted_iota(jnp.int32, (ROWS, ROWS), 0) == lax.broadcasted_iota(
        jnp.int32, (ROWS, ROWS), 1
    )
    gain_bf = gain[...].astype(BF16).astype(F32)
    column = jnp.sum(jnp.where(eye, gain_bf, 0.0), axis=1, keepdims=True)
    w = weight[0]
    gw[0, 0, 0, half, :] = (column * w.astype(BF16).astype(F32)).astype(BF16)
    diffs[isl] = (outer[...] - w).astype(BF16)

    def send_far(k):
        remote(
            gw.at[0, 0, 0, half], gw.at[4 - k, 0, 0, half], g_send.at[0], gh_recv.at[4 - k], far[k]
        ).start()

    def wait_far(k):
        await_recv(gw.at[k, 0, 0, half], gh_recv.at[k])

    def send_near(k):
        for j, d in ((2, 2), (3, 1), (1, -1)):
            remote(
                gw.at[k, 0, 0, half], gw.at[k, 0, j, half], g_send.at[1], gz_recv.at[k, j], near[d]
            ).start()

    def send_x(k, q):
        block = gw.at[k, q, :, half]
        remote(block, block, g_send.at[4], gx_recv.at[k, q], partner).start()

    def send_y(k):
        for j in (1, 3, 2):
            await_recv(gw.at[k, 0, j, half], gz_recv.at[k, j])
        block = gw.at[k, 0, :, half]
        remote(block, gw.at[k, 3, :, half], g_send.at[2], gy_recv.at[k, 3], up_y).start()
        remote(block, gw.at[k, 1, :, half], g_send.at[2], gy_recv.at[k, 1], down_y).start()
        send_x(k, 0)

    def forward_y(k):
        await_recv(gw.at[k, 3, :, half], gy_recv.at[k, 3])
        remote(
            gw.at[k, 3, first, half], gw.at[k, 2, first, half], g_send.at[3], gy_recv.at[k, 0], up_y
        ).start()
        await_recv(gw.at[k, 1, :, half], gy_recv.at[k, 1])
        remote(
            gw.at[k, 1, last, half], gw.at[k, 2, last, half], g_send.at[3], gy_recv.at[k, 2], down_y
        ).start()
        send_x(k, 3)
        send_x(k, 1)

    def opposite(k):
        await_recv(gw.at[k, 2, first, half], gy_recv.at[k, 0])
        await_recv(gw.at[k, 2, last, half], gy_recv.at[k, 2])
        send_x(k, 2)

    def keys_part(k, q):
        await_recv(gw.at[k, q, :, other], gx_recv.at[k, q])
        columns = pl.ds(q * 4 * BLOCK, 4 * BLOCK)
        acc[...] += jnp.dot(
            xv[k, :, columns], gw[k, q].reshape(4 * BLOCK, HEAD), preferred_element_type=F32
        )

    def block_of(k, q, j):
        lanes = (q * 4 + j) * BLOCK
        return part[k, :, lanes : lanes + BLOCK]

    def step_one(k):
        part[k] = jnp.dot(kgt[...], xv[k], preferred_element_type=F32)
        for j in range(4):
            s_a[k, j] = block_of(k, 2, j).astype(BF16)
        remote(s_a.at[k, first], r_a.at[k, first], rs_send.at[0], a_recv.at[k, 0], up_y).start()
        remote(s_a.at[k, last], r_a.at[k, last], rs_send.at[0], a_recv.at[k, 1], down_y).start()

    def step_two(k):
        await_recv(r_a.at[k, first], a_recv.at[k, 0])
        for j in range(4):
            mine = block_of(k, 1, j)
            s_bp[k, j] = (mine + r_a[k, j].astype(F32) if j < 2 else mine).astype(BF16)
        remote(s_bp.at[k], r_bp.at[k], rs_send.at[1], b_recv.at[k, 0], up_y).start()
        await_recv(r_a.at[k, last], a_recv.at[k, 1])
        for j in range(4):
            mine = block_of(k, 3, j)
            s_bm[k, j] = (mine if j < 2 else mine + r_a[k, j].astype(F32)).astype(BF16)
        remote(s_bm.at[k], r_bm.at[k], rs_send.at[2], b_recv.at[k, 1], down_y).start()

    def step_three(k):
        await_recv(r_bp.at[k], b_recv.at[k, 0])
        await_recv(r_bm.at[k], b_recv.at[k, 1])
        for j in (2, 1, 3, 0):
            summed = block_of(k, 0, j) + r_bp[k, j].astype(F32) + r_bm[k, j].astype(F32)
            if j == 0:
                own[k] = summed
            else:
                s_z[k, j - 1] = summed.astype(BF16)
                remote(
                    s_z.at[k, j - 1],
                    r_z.at[k, j - 1],
                    rs_send.at[3],
                    z_recv.at[k, j - 1],
                    near[ZSTEP[j]],
                ).start()

    def step_four(k):
        summed = own[k]
        for j in range(3):
            await_recv(r_z.at[k, j], z_recv.at[k, j])
            summed = summed + r_z[k, j].astype(F32)
        if k == 0:
            own[0] = summed
        else:
            s_h[k] = summed.astype(BF16)
            remote(s_h.at[k], r_h.at[k], rs_send.at[4], h_recv.at[k], far[k]).start()

    inv[...] = jnp.zeros_like(inv)
    acc[...] = jnp.zeros_like(acc)
    for k in ORDER:
        await_recv(xv.at[k], sem_x.at[k])

        def squares(q, carry):
            for j in range(4):
                lanes = pl.ds(pl.multiple_of((q * 4 + j) * BLOCK, BLOCK), BLOCK)
                v = xv[k, :, lanes].astype(F32)
                inv[...] += v * v
            return carry

        lax.fori_loop(0, NY, squares, 0)
    scale = lax.rsqrt(jnp.sum(inv[...], axis=1, keepdims=True) * (1.0 / WIDTH) + NORM_EPS)
    inv[...] = jnp.broadcast_to(scale, inv.shape)
    loads[3].wait()
    kgt[...] = (kg[...].astype(F32) * inv[...]).T.astype(BF16)

    pl.semaphore_wait(barrier, len(peers))
    for k in (2, 1, 3):
        send_far(k)
    send_near(0)
    for k in range(1, NI):
        remote(
            diffs.at[isl], diffs.at[isl], d_send.at[k], d_recv.at[NI - k], islands[k - 1]
        ).start()

    for k in ORDER:
        step_one(k)
    send_y(0)
    wait_far(1)
    send_near(1)
    wait_far(3)
    send_near(3)
    step_two(2)
    wait_far(2)
    send_near(2)
    step_two(1)
    send_y(1)
    step_two(3)
    step_two(0)
    forward_y(0)
    send_y(3)
    step_three(2)
    forward_y(1)
    keys_part(0, 0)
    step_three(1)
    send_y(2)
    step_four(2)
    opposite(0)
    keys_part(1, 0)
    forward_y(3)
    step_three(3)
    keys_part(3, 0)
    opposite(1)
    step_four(1)
    step_three(0)
    forward_y(2)
    keys_part(2, 0)
    keys_part(0, 3)
    keys_part(0, 1)
    opposite(3)
    keys_part(1, 3)
    keys_part(1, 1)
    step_four(3)
    opposite(2)
    keys_part(3, 3)
    keys_part(3, 1)
    step_four(0)
    keys_part(2, 3)
    keys_part(2, 1)
    keys_part(0, 2)
    keys_part(1, 2)

    for k in (1, 2, 3):
        await_recv(r_h.at[k], h_recv.at[k])
    total[...] = (
        own[0] + r_h[1].astype(F32) + r_h[2].astype(F32) + r_h[3].astype(F32)
    ).T
    remote(total.at[other], r_x, tail_send, tail_recv, partner).start()

    for k in (3, 2):
        keys_part(k, 2)
    keys_out[...] = acc[...] * (inv[...] * WIDTH ** (-0.5))
    for k in range(1, NI):
        await_recv(diffs.at[(isl + k) % NI], d_recv.at[k])
    summed = diffs[0].astype(F32)
    for k in range(1, NI):
        summed = summed + diffs[k].astype(F32)
    drift_out[...] = summed * (1.0 / NI)

    await_recv(gw.at[pl.ds(1, 3), 0, 0, half], g_send.at[0])
    await_recv(gw.at[:, 0, pl.ds(1, 3), half], g_send.at[1])
    await_recv(gw.at[:, first, :, half], g_send.at[2])
    await_recv(gw.at[:, 2, :, half], g_send.at[3])
    await_recv(gw.at[:, :, :, half], g_send.at[4])
    for k in range(1, NI):
        await_recv(diffs.at[0], d_send.at[k])
    await_recv(s_a, rs_send.at[0])
    await_recv(s_bp, rs_send.at[1])
    await_recv(s_bm, rs_send.at[2])
    await_recv(s_z, rs_send.at[3])
    await_recv(s_h.at[pl.ds(1, 3)], rs_send.at[4])
    await_recv(total.at[other], tail_send)

    await_recv(r_x, tail_recv)
    usum_out[...] = total[half, :] + r_x[...]


def adam_step(param, grad, first, second):
    first = BETA_ONE * first + (1.0 - BETA_ONE) * grad
    second = BETA_TWO * second + (1.0 - BETA_TWO) * grad * grad
    param = param - INNER_LR * (first / (jnp.sqrt(second) + ADAM_EPS) + DECAY * param)
    return (param, first, second)


def update(
    keys,
    unit_sum,
    drift,
    weight,
    weight_m,
    weight_v,
    gain,
    gain_m,
    gain_v,
    outer,
    momentum,
    fragment,
    active,
    keys_out,
    weight_out,
    weight_m_out,
    weight_v_out,
    gain_out,
    gain_m_out,
    gain_v_out,
    outer_out,
    momentum_out,
):
    key_scale = WIDTH ** (-0.5)
    eye = lax.broadcasted_iota(jnp.int32, (ROWS, ROWS), 0) == lax.broadcasted_iota(
        jnp.int32, (ROWS, ROWS), 1
    )

    def to_column(row):
        return jnp.sum(jnp.where(eye, row, jnp.zeros_like(row)), axis=1, keepdims=True)

    keys_out[...] = keys[...].astype(BF16)
    w, sums = weight[0], unit_sum[...]
    gain_bf = gain[...].astype(BF16).astype(F32)
    weight_grad = key_scale * to_column(gain_bf) * sums
    column = jnp.sum(w.astype(BF16).astype(F32) * sums, axis=1, keepdims=True)
    gain_grad = key_scale * jnp.sum(jnp.where(eye, column, 0.0), axis=0, keepdims=True)
    inner, first, second = adam_step(w, weight_grad, weight_m[0], weight_v[0])
    weight_m_out[0], weight_v_out[0] = first, second
    new, first, second = adam_step(gain[...], gain_grad, gain_m[...], gain_v[...])
    gain_out[...], gain_m_out[...], gain_v_out[...] = new, first, second
    pushed = OUTER_MU * momentum[...] + drift[...]
    candidate = outer[...] - OUTER_LR * (OUTER_MU * pushed + drift[...])
    current = lax.rem(active[0], NFRAG)
    chosen = jnp.where(fragment[...] == current, 1.0, 0.0)
    in_fragment = jnp.broadcast_to(to_column(chosen), (ROWS, HEAD)) > 0.5
    momentum_out[...] = jnp.where(in_fragment, pushed, momentum[...])
    outer_out[...] = jnp.where(in_fragment, candidate, outer[...])
    weight_out[0] = jnp.where(
        in_fragment, MIX_KEEP * inner + (1.0 - MIX_KEEP) * candidate, inner
    )


def shards(
    tokens,
    key_grad,
    weight,
    weight_m,
    weight_v,
    gain,
    gain_m,
    gain_v,
    outer,
    momentum,
    fragment_of_row,
    active_fragment,
):
    vmem = pl.BlockSpec(memory_space=pltpu.VMEM)
    block = (HEAD, BLOCK)
    dma = pltpu.SemaphoreType.DMA
    keys, unit_sum, outer_drift = pl.pallas_call(
        exchange,
        out_shape=(
            pltpu.VMEM((TOK, HEAD), F32),
            pltpu.VMEM((ROWS, HEAD), F32),
            pltpu.VMEM((ROWS, HEAD), F32),
        ),
        in_specs=[pl.BlockSpec(memory_space=pl.ANY)] * 5,
        out_specs=(vmem, vmem, vmem),
        scratch_shapes=[
            pltpu.VMEM((4, TOK, GROUP), BF16),
            pltpu.VMEM((4, NY, 4, BLOCK, HEAD), BF16),
            pltpu.VMEM((4, HEAD, GROUP), F32),
            *[pltpu.VMEM((4, 4) + block, BF16)] * 6,
            *[pltpu.VMEM((4, 3) + block, BF16)] * 2,
            *[pltpu.VMEM((4,) + block, BF16)] * 2,
            pltpu.VMEM((4,) + block, F32),
            pltpu.VMEM(block, F32),
            pltpu.VMEM((ROWS, HEAD), F32),
            pltpu.VMEM((NI, ROWS, HEAD), BF16),
            pltpu.VMEM((TOK, HEAD), F32),
            pltpu.VMEM((HEAD, TOK), BF16),
            pltpu.VMEM((TOK, HEAD), F32),
            pltpu.VMEM((TOK, HEAD), BF16),
            pltpu.VMEM((1, ROWS, HEAD), F32),
            pltpu.VMEM((1, ROWS), F32),
            pltpu.VMEM((ROWS, HEAD), F32),
            dma((4,)),
            dma((4,)),
            dma((4,)),
            dma((4, 4)),
            dma((4, 4)),
            dma((4, 4)),
            dma((5,)),
            dma((4, 2)),
            dma((4, 2)),
            dma((4, 3)),
            dma((4,)),
            dma((5,)),
            dma,
            dma,
            dma((NI,)),
            dma((NI,)),
        ],
        compiler_params=pltpu.CompilerParams(
            collective_id=0, has_side_effects=True, vmem_limit_bytes=60 * 2**20
        ),
        cost_estimate=pl.CostEstimate(
            flops=4 * TOK * WIDTH * HEAD, bytes_accessed=2 * TOK * WIDTH, transcendentals=0
        ),
    )(tokens, key_grad, weight, gain, outer)
    state = (ROWS, HEAD)
    results = pl.pallas_call(
        update,
        out_shape=(
            jax.ShapeDtypeStruct((TOK, HEAD), BF16),
            jax.ShapeDtypeStruct((1,) + state, F32),
            jax.ShapeDtypeStruct((1,) + state, F32),
            jax.ShapeDtypeStruct((1,) + state, F32),
            jax.ShapeDtypeStruct((1, ROWS), F32),
            jax.ShapeDtypeStruct((1, ROWS), F32),
            jax.ShapeDtypeStruct((1, ROWS), F32),
            jax.ShapeDtypeStruct(state, F32),
            jax.ShapeDtypeStruct(state, F32),
        ),
        in_specs=[vmem] * 12 + [pl.BlockSpec(memory_space=pltpu.SMEM)],
        out_specs=(vmem,) * 9,
        compiler_params=pltpu.CompilerParams(vmem_limit_bytes=4 * 2**20),
    )(
        keys,
        unit_sum,
        outer_drift,
        weight,
        weight_m,
        weight_v,
        gain,
        gain_m,
        gain_v,
        outer,
        momentum,
        fragment_of_row[None],
        active_fragment,
    )
    return results


def solution(mesh):
    return jax.shard_map(
        shards,
        mesh=mesh,
        in_specs=(
            P(("island", "fsdp"), None),
            P(("island", "fsdp"), None),
            P("island", "fsdp", None),
            P("island", "fsdp", None),
            P("island", "fsdp", None),
            P("island", "fsdp"),
            P("island", "fsdp"),
            P("island", "fsdp"),
            P("fsdp", None),
            P("fsdp", None),
            P("fsdp"),
            P(),
        ),
        out_specs=(
            P(("island", "fsdp"), None),
            P("island", "fsdp", None),
            P("island", "fsdp", None),
            P("island", "fsdp", None),
            P("island", "fsdp"),
            P("island", "fsdp"),
            P("island", "fsdp"),
            P("fsdp", None),
            P("fsdp", None),
        ),
        check_vma=False,
    )
```

time: 1280 us -> 58.1 us (0.05)
  blocking collectives: 1230 us -> 0 us
  Pallas kernels: 0 us -> 56 us
  between operations: 15.5 us -> 1.49 us
    psum x2 -> x0, blocking collectives: 621 us -> none  [the longest x1 607 us: shards(): gain_total = lax.psum(gain_term, 'fsdp')]
    unnamed x1 -> x0, blocking collectives: 611 us -> none
    pallas_call x0 -> x2, Pallas kernels: none -> 56 us  [the longest x1 55.2 us: shards(): pl.pallas_call(exchange, out_shape=(pltpu.VMEM((TOK, HEAD), F32), pltpu.V...]
  transfers between devices with their start and end apart: 2 -> 0, of which waited for: 0 -> 0; matrix products, arithmetic and copies ran while one was open for 2% -> 0% of each run, Pallas kernels for 0% -> 0%
where the time goes in v2:
time: 58.1 us; the launch traced here: 57.5 us
  Pallas kernels  56 us (96%)
  between operations  1.49 us (3%)
    pallas_call x1, Pallas kernels, shards(): pl.pallas_call(exchange, out_shape=(pltpu.VMEM((TOK, HEAD), F32), pltpu.V...  55.2 us

profile of v2, /device:TPU:6, one launch (start us, length us, event | category | flops | bytes accessed | tf_op | source)
XLA Modules:
  0.0 57.5 jit_solution(18034694250712556252)
XLA Ops:
  0.6 0.0 copy-start.1
  0.7 0.0 copy-start.5
  0.7 0.0 copy-start
  0.7 0.0 copy-start.8
  0.7 0.0 copy-start.4
  0.7 0.0 copy-start.7
  0.7 0.0 copy-start.6
  0.7 0.0 copy-start.3
  0.7 0.0 copy-start.2
  1.4 55.2 %shard_map.187 = (f32[256,128]{1,0:T(8,128)S(1)}, f32[64,128]{1,0:T(8,128)S(1)}, f32[64,128]{1,0:T(8,128)S(1)}) custom-call(bf16[256,8192]{1,0:T(8,128)(2,1)} %x_hbm.1, bf16[256,128]{1,0:T(8,128)(2,1)} %kg_hbm.1, f32[1,64,128]{2,1,0:T(8,128)} %weight.1, f32[1,64]{1,0:T(1,128)} %gain.1, f32[64,128]{1,0:T(8,128)} %outer.1), custom_call_target="tpu_custom_call" | custom-call | flops 1073741824 | bytes 4194304 | tf_op jit(solution)/shard_map/pallas_call | solution.py:439
  56.6 0.0 copy-done.1
  56.6 0.0 copy-done.5
  56.6 0.0 copy-done
  56.6 0.0 copy-done.8
  56.7 0.0 copy-done.4
  56.7 0.0 copy-done.7
  56.7 0.0 copy-done.6
  56.7 0.0 copy-done.3
  56.7 0.0 copy-done.2
  56.7 0.8 %shard_map.188 = (bf16[256,128]{1,0:T(8,128)(2,1)}, f32[1,64,128]{2,1,0:T(8,128)}, f32[1,64,128]{2,1,0:T(8,128)}, f32[1,64,128]{2,1,0:T(8,128)}, f32[1,64]{1,0:T...) custom-call(f32[256,128]{1,0:T(8,128)S(1)} %get-tuple-element.12.keys, ...), custom_call_target="tpu_custom_call" | custom-call | tf_op jit(solution)/shard_map/pallas_call | solution.py:491
Async XLA Ops:
  0.6 56.0 %copy-start.1 = (f32[64,128]{1,0:T(8,128)S(1)}, f32[64,128]{1,0:T(8,128)}, u32[]{:S(2)}) copy-start(f32[64,128]{1,0:T(8,128)} %outer.1) | copy-start | bytes 98308
  0.7 56.0 %copy-start.5 = (f32[1,64]{1,0:T(1,128)S(1)}, f32[1,64]{1,0:T(1,128)}, u32[]{:S(2)}) copy-start(f32[1,64]{1,0:T(1,128)} %gain.1) | copy-start | bytes 772
  0.7 56.0 %copy-start = (f32[1,64,128]{2,1,0:T(8,128)S(1)}, f32[1,64,128]{2,1,0:T(8,128)}, u32[]{:S(2)}) copy-start(f32[1,64,128]{2,1,0:T(8,128)} %weight.1) | copy-start | bytes 98308
  0.7 56.0 %copy-start.8 = (s32[64]{0:T(128)S(1)}, s32[64]{0:T(128)}, u32[]{:S(2)}) copy-start(s32[64]{0:T(128)} %param.22) | copy-start | bytes 772
  0.7 56.0 %copy-start.4 = (f32[64,128]{1,0:T(8,128)S(1)}, f32[64,128]{1,0:T(8,128)}, u32[]{:S(2)}) copy-start(f32[64,128]{1,0:T(8,128)} %momentum.1) | copy-start | bytes 98308
  0.7 56.0 %copy-start.7 = (f32[1,64]{1,0:T(1,128)S(1)}, f32[1,64]{1,0:T(1,128)}, u32[]{:S(2)}) copy-start(f32[1,64]{1,0:T(1,128)} %gain_v.1) | copy-start | bytes 772
  0.7 56.0 %copy-start.6 = (f32[1,64]{1,0:T(1,128)S(1)}, f32[1,64]{1,0:T(1,128)}, u32[]{:S(2)}) copy-start(f32[1,64]{1,0:T(1,128)} %gain_m.1) | copy-start | bytes 772
  0.7 56.0 %copy-start.3 = (f32[1,64,128]{2,1,0:T(8,128)S(1)}, f32[1,64,128]{2,1,0:T(8,128)}, u32[]{:S(2)}) copy-start(f32[1,64,128]{2,1,0:T(8,128)} %weight_v.1) | copy-start | bytes 98308
  0.7 56.0 %copy-start.2 = (f32[1,64,128]{2,1,0:T(8,128)S(1)}, f32[1,64,128]{2,1,0:T(8,128)}, u32[]{:S(2)}) copy-start(f32[1,64,128]{2,1,0:T(8,128)} %weight_m.1) | copy-start | bytes 98308

commit v3 on v2

--- a/solution.py
+++ b/solution.py
@@ -22,6 +22,8 @@
 ROWS = 64
 BLOCK = NX * ROWS
 ZSTEP = (0, 1, -2, -1)
+EARLY = 16
+DIRECT = 2
 ORDER = (2, 1, 3, 0)
 GROUP = NY * 4 * BLOCK
 F32, BF16 = jnp.float32, jnp.bfloat16
@@ -48,10 +50,9 @@
     s_z,
     r_z,
     s_h,
-    r_h,
     own,
-    total,
-    r_x,
+    s_o,
+    r_t,
     diffs,
     acc,
     kgt,
@@ -66,14 +67,16 @@
     gz_recv,
     gy_recv,
     gx_recv,
+    ty_recv,
+    th_recv,
+    tz_recv,
     g_send,
     a_recv,
     b_recv,
     z_recv,
-    h_recv,
     rs_send,
     tail_send,
-    tail_recv,
+    t_recv,
     d_send,
     d_recv,
 ):
@@ -96,11 +99,16 @@
     up_y, down_y = device(dy=1), device(dy=-1)
     near = {d: device(dz=d) for d in (1, -1, 2, -2)}
     far = {k: device(dz=d) for k, d in ((1, 4), (2, 8), (3, -4))}
+    near_flip = {d: device(dz=d, flip=True) for d in (1, -1, 2, -2)}
+    far_flip = {k: device(dz=d, flip=True) for k, d in ((1, 4), (2, 8), (3, -4))}
+    opposite_y = device(dy=2)
     partner = device(flip=True)
     islands = [((isl + k) % NI, f) for k in range(1, NI)]
 
     barrier = pltpu.get_barrier_semaphore()
-    peers = [up_y, down_y, partner] + list(near.values()) + list(far.values()) + islands
+    peers = [up_y, down_y, opposite_y, partner] + islands
+    for group in (near, far, near_flip, far_flip):
+        peers += list(group.values())
     for peer in peers:
         pl.semaphore_signal(barrier, inc=1, device_id=peer, device_id_type=MESH)
 
@@ -135,6 +143,8 @@
 
     half = pl.ds(pl.multiple_of(xl * ROWS, ROWS), ROWS)
     other = pl.ds(pl.multiple_of((1 - xl) * ROWS, ROWS), ROWS)
+    main = pl.ds(pl.multiple_of(xl * ROWS, ROWS), ROWS - EARLY)
+    early = pl.ds(pl.multiple_of(xl * ROWS + ROWS - EARLY, EARLY), EARLY)
     first, last = pl.ds(0, 2), pl.ds(2, 2)
 
     for copy in loads[:3]:
@@ -150,17 +160,50 @@
 
     def send_far(k):
         remote(
-            gw.at[0, 0, 0, half], gw.at[4 - k, 0, 0, half], g_send.at[0], gh_recv.at[4 - k], far[k]
+            gw.at[0, 0, 0, main], gw.at[4 - k, 0, 0, main], g_send.at[0], gh_recv.at[4 - k], far[k]
         ).start()
 
     def wait_far(k):
-        await_recv(gw.at[k, 0, 0, half], gh_recv.at[k])
+        await_recv(gw.at[k, 0, 0, main], gh_recv.at[k])
 
     def send_near(k):
         for j, d in ((2, 2), (3, 1), (1, -1)):
             remote(
-                gw.at[k, 0, 0, half], gw.at[k, 0, j, half], g_send.at[1], gz_recv.at[k, j], near[d]
+                gw.at[k, 0, 0, main], gw.at[k, 0, j, main], g_send.at[1], gz_recv.at[k, j], near[d]
             ).start()
+
+    def early_y():
+        mine = gw.at[0, 0, 0, early]
+        for q, to in ((3, up_y), (1, down_y), (2, opposite_y)):
+            remote(mine, gw.at[0, q, 0, early], g_send.at[5], ty_recv.at[q], to).start()
+
+    def early_near(k):
+        for j, d in ((2, 2), (3, 1), (1, -1)):
+            remote(
+                gw.at[k, :, 0, early], gw.at[k, :, j, early], g_send.at[7], tz_recv.at[k, j], near[d]
+            ).start()
+
+    def early_z():
+        for q in (1, 2, 3):
+            await_recv(gw.at[0, q, 0, early], ty_recv.at[q])
+        for k in (2, 1, 3):
+            remote(
+                gw.at[0, :, 0, early],
+                gw.at[4 - k, :, 0, early],
+                g_send.at[6],
+                th_recv.at[4 - k],
+                far[k],
+            ).start()
+        early_near(0)
+
+    def early_far(k):
+        await_recv(gw.at[k, :, 0, early], th_recv.at[k])
+        early_near(k)
+
+    def early_x(k):
+        for j in (1, 2, 3):
+            await_recv(gw.at[k, :, j, early], tz_recv.at[k, j])
+        send_x(k, 0)
 
     def send_x(k, q):
         block = gw.at[k, q, :, half]
@@ -168,27 +211,34 @@
 
     def send_y(k):
         for j in (1, 3, 2):
-            await_recv(gw.at[k, 0, j, half], gz_recv.at[k, j])
-        block = gw.at[k, 0, :, half]
-        remote(block, gw.at[k, 3, :, half], g_send.at[2], gy_recv.at[k, 3], up_y).start()
-        remote(block, gw.at[k, 1, :, half], g_send.at[2], gy_recv.at[k, 1], down_y).start()
-        send_x(k, 0)
+            await_recv(gw.at[k, 0, j, main], gz_recv.at[k, j])
+        block = gw.at[k, 0, :, main]
+        remote(block, gw.at[k, 3, :, main], g_send.at[2], gy_recv.at[k, 3], up_y).start()
+        remote(block, gw.at[k, 1, :, main], g_send.at[2], gy_recv.at[k, 1], down_y).start()
+        if k == DIRECT:
+            remote(
+                block, gw.at[k, 2, :, main], g_send.at[3], gy_recv.at[k, 2], opposite_y
+            ).start()
 
     def forward_y(k):
-        await_recv(gw.at[k, 3, :, half], gy_recv.at[k, 3])
-        remote(
-            gw.at[k, 3, first, half], gw.at[k, 2, first, half], g_send.at[3], gy_recv.at[k, 0], up_y
-        ).start()
-        await_recv(gw.at[k, 1, :, half], gy_recv.at[k, 1])
-        remote(
-            gw.at[k, 1, last, half], gw.at[k, 2, last, half], g_send.at[3], gy_recv.at[k, 2], down_y
-        ).start()
-        send_x(k, 3)
-        send_x(k, 1)
+        for q, part_j, slot, to in ((3, first, 0, up_y), (1, last, 2, down_y)):
+            await_recv(gw.at[k, q, :, main], gy_recv.at[k, q])
+            if k != DIRECT:
+                remote(
+                    gw.at[k, q, part_j, main],
+                    gw.at[k, 2, part_j, main],
+                    g_send.at[3],
+                    gy_recv.at[k, slot],
+                    to,
+                ).start()
+            send_x(k, q)
 
     def opposite(k):
-        await_recv(gw.at[k, 2, first, half], gy_recv.at[k, 0])
-        await_recv(gw.at[k, 2, last, half], gy_recv.at[k, 2])
+        if k == DIRECT:
+            await_recv(gw.at[k, 2, :, main], gy_recv.at[k, 2])
+        else:
+            await_recv(gw.at[k, 2, first, main], gy_recv.at[k, 0])
+            await_recv(gw.at[k, 2, last, main], gy_recv.at[k, 2])
         send_x(k, 2)
 
     def keys_part(k, q):
@@ -199,11 +249,13 @@
         )
 
     def block_of(k, q, j):
-        lanes = (q * 4 + j) * BLOCK
-        return part[k, :, lanes : lanes + BLOCK]
+        start = (q * 4 + j) * BLOCK
+        return part[k, start : start + BLOCK]
 
     def step_one(k):
-        part[k] = jnp.dot(kgt[...], xv[k], preferred_element_type=F32)
+        part[k] = lax.dot_general(
+            xv[k], kgt[...], (((0,), (0,)), ((), ())), preferred_element_type=F32
+        )
         for j in range(4):
             s_a[k, j] = block_of(k, 2, j).astype(BF16)
         remote(s_a.at[k, first], r_a.at[k, first], rs_send.at[0], a_recv.at[k, 0], up_y).start()
@@ -221,6 +273,10 @@
             s_bm[k, j] = (mine if j < 2 else mine + r_a[k, j].astype(F32)).astype(BF16)
         remote(s_bm.at[k], r_bm.at[k], rs_send.at[2], b_recv.at[k, 1], down_y).start()
 
+    def split(block, place, send, key, same, flipped):
+        for rows, slot, to in ((half, place, same[key]), (other, place + 1, flipped[key])):
+            remote(block.at[rows], r_t.at[slot], send, t_recv.at[slot], to).start()
+
     def step_three(k):
         await_recv(r_bp.at[k], b_recv.at[k, 0])
         await_recv(r_bm.at[k], b_recv.at[k, 1])
@@ -228,8 +284,14 @@
             summed = block_of(k, 0, j) + r_bp[k, j].astype(F32) + r_bm[k, j].astype(F32)
             if j == 0:
                 own[k] = summed
+                if k == 0:
+                    s_o[...] = summed.astype(BF16)
+                    remote(s_o.at[other], r_t.at[12], tail_send, t_recv.at[12], partner).start()
+                continue
+            s_z[k, j - 1] = summed.astype(BF16)
+            if k == 0:
+                split(s_z.at[0, j - 1], 2 * j - 2, rs_send.at[3], ZSTEP[j], near, near_flip)
             else:
-                s_z[k, j - 1] = summed.astype(BF16)
                 remote(
                     s_z.at[k, j - 1],
                     r_z.at[k, j - 1],
@@ -243,11 +305,8 @@
         for j in range(3):
             await_recv(r_z.at[k, j], z_recv.at[k, j])
             summed = summed + r_z[k, j].astype(F32)
-        if k == 0:
-            own[0] = summed
-        else:
-            s_h[k] = summed.astype(BF16)
-            remote(s_h.at[k], r_h.at[k], rs_send.at[4], h_recv.at[k], far[k]).start()
+        s_h[k] = summed.astype(BF16)
+        split(s_h.at[k], 4 + 2 * k, rs_send.at[4], k, far, far_flip)
 
     inv[...] = jnp.zeros_like(inv)
     acc[...] = jnp.zeros_like(acc)
@@ -265,9 +324,10 @@
     scale = lax.rsqrt(jnp.sum(inv[...], axis=1, keepdims=True) * (1.0 / WIDTH) + NORM_EPS)
     inv[...] = jnp.broadcast_to(scale, inv.shape)
     loads[3].wait()
-    kgt[...] = (kg[...].astype(F32) * inv[...]).T.astype(BF16)
+    kgt[...] = (kg[...].astype(F32) * inv[...]).astype(BF16)
 
     pl.semaphore_wait(barrier, len(peers))
+    early_y()
     for k in (2, 1, 3):
         send_far(k)
     send_near(0)
@@ -279,6 +339,7 @@
     for k in ORDER:
         step_one(k)
     send_y(0)
+    early_z()
     wait_far(1)
     send_near(1)
     wait_far(3)
@@ -287,51 +348,50 @@
     wait_far(2)
     send_near(2)
     step_two(1)
+    early_x(0)
     send_y(1)
+    send_y(3)
+    early_far(1)
+    early_far(3)
+    forward_y(0)
+    send_y(2)
+    early_far(2)
     step_two(3)
+    early_x(1)
+    early_x(3)
+    early_x(2)
+    forward_y(1)
+    forward_y(3)
     step_two(0)
-    forward_y(0)
-    send_y(3)
     step_three(2)
-    forward_y(1)
+    opposite(0)
+    forward_y(2)
+    step_three(1)
+    step_four(2)
+    opposite(1)
+    opposite(3)
+    opposite(2)
+    step_three(3)
+    step_four(1)
     keys_part(0, 0)
-    step_three(1)
-    send_y(2)
-    step_four(2)
-    opposite(0)
+    keys_part(0, 1)
+    keys_part(0, 3)
     keys_part(1, 0)
-    forward_y(3)
-    step_three(3)
     keys_part(3, 0)
-    opposite(1)
-    step_four(1)
+    keys_part(2, 0)
     step_three(0)
-    forward_y(2)
-    keys_part(2, 0)
-    keys_part(0, 3)
-    keys_part(0, 1)
-    opposite(3)
+    step_four(3)
+    keys_part(1, 1)
     keys_part(1, 3)
-    keys_part(1, 1)
-    step_four(3)
-    opposite(2)
+    keys_part(3, 1)
     keys_part(3, 3)
-    keys_part(3, 1)
-    step_four(0)
+    keys_part(0, 2)
+    keys_part(2, 1)
     keys_part(2, 3)
-    keys_part(2, 1)
-    keys_part(0, 2)
     keys_part(1, 2)
-
-    for k in (1, 2, 3):
-        await_recv(r_h.at[k], h_recv.at[k])
-    total[...] = (
-        own[0] + r_h[1].astype(F32) + r_h[2].astype(F32) + r_h[3].astype(F32)
-    ).T
-    remote(total.at[other], r_x, tail_send, tail_recv, partner).start()
-
-    for k in (3, 2):
-        keys_part(k, 2)
+    keys_part(3, 2)
+    keys_part(2, 2)
+
     keys_out[...] = acc[...] * (inv[...] * WIDTH ** (-0.5))
     for k in range(1, NI):
         await_recv(diffs.at[(isl + k) % NI], d_recv.at[k])
@@ -340,11 +400,14 @@
         summed = summed + diffs[k].astype(F32)
     drift_out[...] = summed * (1.0 / NI)
 
-    await_recv(gw.at[pl.ds(1, 3), 0, 0, half], g_send.at[0])
-    await_recv(gw.at[:, 0, pl.ds(1, 3), half], g_send.at[1])
-    await_recv(gw.at[:, first, :, half], g_send.at[2])
-    await_recv(gw.at[:, 2, :, half], g_send.at[3])
+    await_recv(gw.at[pl.ds(1, 3), 0, 0, main], g_send.at[0])
+    await_recv(gw.at[:, 0, pl.ds(1, 3), main], g_send.at[1])
+    await_recv(gw.at[:, first, :, main], g_send.at[2])
+    await_recv(gw.at[:, 2, :, main], g_send.at[3])
     await_recv(gw.at[:, :, :, half], g_send.at[4])
+    await_recv(gw.at[0, pl.ds(1, 3), 0, early], g_send.at[5])
+    await_recv(gw.at[pl.ds(1, 3), :, 0, early], g_send.at[6])
+    await_recv(gw.at[:, :, pl.ds(1, 3), early], g_send.at[7])
     for k in range(1, NI):
         await_recv(diffs.at[0], d_send.at[k])
     await_recv(s_a, rs_send.at[0])
@@ -352,10 +415,13 @@
     await_recv(s_bm, rs_send.at[2])
     await_recv(s_z, rs_send.at[3])
     await_recv(s_h.at[pl.ds(1, 3)], rs_send.at[4])
-    await_recv(total.at[other], tail_send)
-
-    await_recv(r_x, tail_recv)
-    usum_out[...] = total[half, :] + r_x[...]
+    await_recv(s_o.at[other], tail_send)
+
+    summed = own[0, half, :]
+    for slot in range(13):
+        await_recv(r_t.at[slot], t_recv.at[slot])
+        summed = summed + r_t[slot].astype(F32)
+    usum_out[...] = summed
 
 
 def adam_step(param, grad, first, second):
@@ -409,7 +475,7 @@
     gain_out[...], gain_m_out[...], gain_v_out[...] = new, first, second
     pushed = OUTER_MU * momentum[...] + drift[...]
     candidate = outer[...] - OUTER_LR * (OUTER_MU * pushed + drift[...])
-    current = lax.rem(active[0], NFRAG)
+    current = lax.rem(active[...], NFRAG)
     chosen = jnp.where(fragment[...] == current, 1.0, 0.0)
     in_fragment = jnp.broadcast_to(to_column(chosen), (ROWS, HEAD)) > 0.5
     momentum_out[...] = jnp.where(in_fragment, pushed, momentum[...])
@@ -448,16 +514,16 @@
         scratch_shapes=[
             pltpu.VMEM((4, TOK, GROUP), BF16),
             pltpu.VMEM((4, NY, 4, BLOCK, HEAD), BF16),
-            pltpu.VMEM((4, HEAD, GROUP), F32),
+            pltpu.VMEM((4, GROUP, HEAD), F32),
             *[pltpu.VMEM((4, 4) + block, BF16)] * 6,
             *[pltpu.VMEM((4, 3) + block, BF16)] * 2,
-            *[pltpu.VMEM((4,) + block, BF16)] * 2,
+            pltpu.VMEM((4,) + block, BF16),
             pltpu.VMEM((4,) + block, F32),
-            pltpu.VMEM(block, F32),
-            pltpu.VMEM((ROWS, HEAD), F32),
+            pltpu.VMEM(block, BF16),
+            pltpu.VMEM((13, ROWS, HEAD), BF16),
             pltpu.VMEM((NI, ROWS, HEAD), BF16),
             pltpu.VMEM((TOK, HEAD), F32),
-            pltpu.VMEM((HEAD, TOK), BF16),
+            pltpu.VMEM((TOK, HEAD), BF16),
             pltpu.VMEM((TOK, HEAD), F32),
             pltpu.VMEM((TOK, HEAD), BF16),
             pltpu.VMEM((1, ROWS, HEAD), F32),
@@ -469,14 +535,16 @@
             dma((4, 4)),
             dma((4, 4)),
             dma((4, 4)),
-            dma((5,)),
+            dma((NY,)),
+            dma((4,)),
+            dma((4, 4)),
+            dma((8,)),
             dma((4, 2)),
             dma((4, 2)),
             dma((4, 3)),
-            dma((4,)),
             dma((5,)),
             dma,
-            dma,
+            dma((13,)),
             dma((NI,)),
             dma((NI,)),
         ],
@@ -501,7 +569,7 @@
             jax.ShapeDtypeStruct(state, F32),
             jax.ShapeDtypeStruct(state, F32),
         ),
-        in_specs=[vmem] * 12 + [pl.BlockSpec(memory_space=pltpu.SMEM)],
+        in_specs=[vmem] * 13,
         out_specs=(vmem,) * 9,
         compiler_params=pltpu.CompilerParams(vmem_limit_bytes=4 * 2**20),
     )(
@@ -517,7 +585,7 @@
         outer,
         momentum,
         fragment_of_row[None],
-        active_fragment,
+        active_fragment[None],
     )
     return results
 

time: 58.1 us -> 56.4 us (0.971)
  Pallas kernels: 56 us -> 54.6 us
    pallas_call x1, Pallas kernels: 55.2 us -> 53.8 us  [shards(): pl.pallas_call(exchange, out_shape=(pltpu.VMEM((TOK, HEAD), F32), pltpu.V...]
where the time goes in v3:
time: 56.4 us; the launch traced here: 56.1 us
  Pallas kernels  54.6 us (97%)
  between operations  1.49 us (3%)
    pallas_call x1, Pallas kernels, shards(): pl.pallas_call(exchange, out_shape=(pltpu.VMEM((TOK, HEAD), F32), pltpu.V...  53.8 us

profile of v3, /device:TPU:6, one launch (start us, length us, event | category | flops | bytes accessed | tf_op | source)
XLA Modules:
  0.0 56.1 jit_solution(4872844365186822098)
XLA Ops:
  0.6 0.0 copy-start.1
  0.7 0.0 copy-start.5
  0.7 0.0 copy-start
  0.7 0.0 copy-start.8
  0.7 0.0 copy-start.4
  0.7 0.0 copy-start.7
  0.7 0.0 copy-start.6
  0.7 0.0 copy-start.3
  0.7 0.0 copy-start.2
  1.4 53.8 %shard_map.187 = (f32[256,128]{1,0:T(8,128)S(1)}, f32[64,128]{1,0:T(8,128)S(1)}, f32[64,128]{1,0:T(8,128)S(1)}) custom-call(bf16[256,8192]{1,0:T(8,128)(2,1)} %x_hbm.1, bf16[256,128]{1,0:T(8,128)(2,1)} %kg_hbm.1, f32[1,64,128]{2,1,0:T(8,128)} %weight.1, f32[1,64]{1,0:T(1,128)} %gain.1, f32[64,128]{1,0:T(8,128)} %outer.1), custom_call_target="tpu_custom_call" | custom-call | flops 1073741824 | bytes 4194304 | tf_op jit(solution)/shard_map/pallas_call | solution.py:505
  55.2 0.0 copy-done.1
  55.2 0.0 copy-done.5
  55.2 0.0 copy-done
  55.2 0.0 copy-done.8
  55.2 0.0 copy-done.4
  55.3 0.0 copy-done.7
  55.3 0.0 copy-done.6
  55.3 0.0 copy-done.3
  55.3 0.0 copy-done.2
  55.3 0.8 %shard_map.188 = (bf16[256,128]{1,0:T(8,128)(2,1)}, f32[1,64,128]{2,1,0:T(8,128)}, f32[1,64,128]{2,1,0:T(8,128)}, f32[1,64,128]{2,1,0:T(8,128)}, f32[1,64]{1,0:T...) custom-call(f32[256,128]{1,0:T(8,128)S(1)} %get-tuple-element.12.keys, ...), custom_call_target="tpu_custom_call" | custom-call | tf_op jit(solution)/shard_map/pallas_call | solution.py:559
Async XLA Ops:
  0.6 54.6 %copy-start.1 = (f32[64,128]{1,0:T(8,128)S(1)}, f32[64,128]{1,0:T(8,128)}, u32[]{:S(2)}) copy-start(f32[64,128]{1,0:T(8,128)} %outer.1) | copy-start | bytes 98308
  0.7 54.6 %copy-start.5 = (f32[1,64]{1,0:T(1,128)S(1)}, f32[1,64]{1,0:T(1,128)}, u32[]{:S(2)}) copy-start(f32[1,64]{1,0:T(1,128)} %gain.1) | copy-start | bytes 772
  0.7 54.6 %copy-start = (f32[1,64,128]{2,1,0:T(8,128)S(1)}, f32[1,64,128]{2,1,0:T(8,128)}, u32[]{:S(2)}) copy-start(f32[1,64,128]{2,1,0:T(8,128)} %weight.1) | copy-start | bytes 98308
  0.7 54.6 %copy-start.8 = (s32[64]{0:T(128)S(1)}, s32[64]{0:T(128)}, u32[]{:S(2)}) copy-start(s32[64]{0:T(128)} %param.22) | copy-start | bytes 772
  0.7 54.6 %copy-start.4 = (f32[64,128]{1,0:T(8,128)S(1)}, f32[64,128]{1,0:T(8,128)}, u32[]{:S(2)}) copy-start(f32[64,128]{1,0:T(8,128)} %momentum.1) | copy-start | bytes 98308
  0.7 54.6 %copy-start.7 = (f32[1,64]{1,0:T(1,128)S(1)}, f32[1,64]{1,0:T(1,128)}, u32[]{:S(2)}) copy-start(f32[1,64]{1,0:T(1,128)} %gain_v.1) | copy-start | bytes 772
  0.7 54.6 %copy-start.6 = (f32[1,64]{1,0:T(1,128)S(1)}, f32[1,64]{1,0:T(1,128)}, u32[]{:S(2)}) copy-start(f32[1,64]{1,0:T(1,128)} %gain_m.1) | copy-start | bytes 772
  0.7 54.6 %copy-start.3 = (f32[1,64,128]{2,1,0:T(8,128)S(1)}, f32[1,64,128]{2,1,0:T(8,128)}, u32[]{:S(2)}) copy-start(f32[1,64,128]{2,1,0:T(8,128)} %weight_v.1) | copy-start | bytes 98308
  0.7 54.6 %copy-start.2 = (f32[1,64,128]{2,1,0:T(8,128)S(1)}, f32[1,64,128]{2,1,0:T(8,128)}, u32[]{:S(2)}) copy-start(f32[1,64,128]{2,1,0:T(8,128)} %weight_m.1) | copy-start | bytes 98308

commit v4 on v3

--- a/solution.py
+++ b/solution.py
@@ -23,7 +23,6 @@
 BLOCK = NX * ROWS
 ZSTEP = (0, 1, -2, -1)
 EARLY = 16
-DIRECT = 2
 ORDER = (2, 1, 3, 0)
 GROUP = NY * 4 * BLOCK
 F32, BF16 = jnp.float32, jnp.bfloat16
@@ -215,30 +214,22 @@
         block = gw.at[k, 0, :, main]
         remote(block, gw.at[k, 3, :, main], g_send.at[2], gy_recv.at[k, 3], up_y).start()
         remote(block, gw.at[k, 1, :, main], g_send.at[2], gy_recv.at[k, 1], down_y).start()
-        if k == DIRECT:
-            remote(
-                block, gw.at[k, 2, :, main], g_send.at[3], gy_recv.at[k, 2], opposite_y
-            ).start()
 
     def forward_y(k):
         for q, part_j, slot, to in ((3, first, 0, up_y), (1, last, 2, down_y)):
             await_recv(gw.at[k, q, :, main], gy_recv.at[k, q])
-            if k != DIRECT:
-                remote(
-                    gw.at[k, q, part_j, main],
-                    gw.at[k, 2, part_j, main],
-                    g_send.at[3],
-                    gy_recv.at[k, slot],
-                    to,
-                ).start()
+            remote(
+                gw.at[k, q, part_j, main],
+                gw.at[k, 2, part_j, main],
+                g_send.at[3],
+                gy_recv.at[k, slot],
+                to,
+            ).start()
             send_x(k, q)
 
     def opposite(k):
-        if k == DIRECT:
-            await_recv(gw.at[k, 2, :, main], gy_recv.at[k, 2])
-        else:
-            await_recv(gw.at[k, 2, first, main], gy_recv.at[k, 0])
-            await_recv(gw.at[k, 2, last, main], gy_recv.at[k, 2])
+        await_recv(gw.at[k, 2, first, main], gy_recv.at[k, 0])
+        await_recv(gw.at[k, 2, last, main], gy_recv.at[k, 2])
         send_x(k, 2)
 
     def keys_part(k, q):
@@ -361,26 +352,26 @@
     early_x(3)
     early_x(2)
     forward_y(1)
+    step_two(0)
     forward_y(3)
-    step_two(0)
     step_three(2)
     opposite(0)
+    step_three(1)
     forward_y(2)
-    step_three(1)
     step_four(2)
     opposite(1)
+    step_three(3)
     opposite(3)
+    step_four(1)
     opposite(2)
-    step_three(3)
-    step_four(1)
+    step_three(0)
+    step_four(3)
     keys_part(0, 0)
     keys_part(0, 1)
     keys_part(0, 3)
     keys_part(1, 0)
     keys_part(3, 0)
     keys_part(2, 0)
-    step_three(0)
-    step_four(3)
     keys_part(1, 1)
     keys_part(1, 3)
     keys_part(3, 1)

time: 56.4 us -> 55.1 us (0.977)
  Pallas kernels: 54.6 us -> 53.2 us
    pallas_call x1, Pallas kernels: 53.8 us -> 52.4 us  [shards(): pl.pallas_call(exchange, out_shape=(pltpu.VMEM((TOK, HEAD), F32), pltpu.V...]
where the time goes in v4:
time: 55.1 us; the launch traced here: 54.8 us
  Pallas kernels  53.2 us (97%)
  between operations  1.49 us (3%)
    pallas_call x1, Pallas kernels, shards(): pl.pallas_call(exchange, out_shape=(pltpu.VMEM((TOK, HEAD), F32), pltpu.V...  52.4 us

profile of v4, /device:TPU:6, one launch (start us, length us, event | category | flops | bytes accessed | tf_op | source)
XLA Modules:
  0.0 54.8 jit_solution(2124964043927143720)
XLA Ops:
  0.6 0.0 copy-start.1
  0.7 0.0 copy-start.5
  0.7 0.0 copy-start
  0.7 0.0 copy-start.8
  0.7 0.0 copy-start.4
  0.7 0.0 copy-start.7
  0.7 0.0 copy-start.6
  0.7 0.0 copy-start.3
  0.7 0.0 copy-start.2
  1.4 52.4 %shard_map.187 = (f32[256,128]{1,0:T(8,128)S(1)}, f32[64,128]{1,0:T(8,128)S(1)}, f32[64,128]{1,0:T(8,128)S(1)}) custom-call(bf16[256,8192]{1,0:T(8,128)(2,1)} %x_hbm.1, bf16[256,128]{1,0:T(8,128)(2,1)} %kg_hbm.1, f32[1,64,128]{2,1,0:T(8,128)} %weight.1, f32[1,64]{1,0:T(1,128)} %gain.1, f32[64,128]{1,0:T(8,128)} %outer.1), custom_call_target="tpu_custom_call" | custom-call | flops 1073741824 | bytes 4194304 | tf_op jit(solution)/shard_map/pallas_call | solution.py:496
  53.8 0.0 copy-done.1
  53.9 0.0 copy-done.5
  53.9 0.0 copy-done
  53.9 0.0 copy-done.8
  53.9 0.0 copy-done.4
  53.9 0.0 copy-done.7
  53.9 0.0 copy-done.6
  53.9 0.0 copy-done.3
  53.9 0.0 copy-done.2
  53.9 0.8 %shard_map.188 = (bf16[256,128]{1,0:T(8,128)(2,1)}, f32[1,64,128]{2,1,0:T(8,128)}, f32[1,64,128]{2,1,0:T(8,128)}, f32[1,64,128]{2,1,0:T(8,128)}, f32[1,64]{1,0:T...) custom-call(f32[256,128]{1,0:T(8,128)S(1)} %get-tuple-element.12.keys, ...), custom_call_target="tpu_custom_call" | custom-call | tf_op jit(solution)/shard_map/pallas_call | solution.py:550
Async XLA Ops:
  0.6 53.2 %copy-start.1 = (f32[64,128]{1,0:T(8,128)S(1)}, f32[64,128]{1,0:T(8,128)}, u32[]{:S(2)}) copy-start(f32[64,128]{1,0:T(8,128)} %outer.1) | copy-start | bytes 98308
  0.7 53.2 %copy-start.5 = (f32[1,64]{1,0:T(1,128)S(1)}, f32[1,64]{1,0:T(1,128)}, u32[]{:S(2)}) copy-start(f32[1,64]{1,0:T(1,128)} %gain.1) | copy-start | bytes 772
  0.7 53.2 %copy-start = (f32[1,64,128]{2,1,0:T(8,128)S(1)}, f32[1,64,128]{2,1,0:T(8,128)}, u32[]{:S(2)}) copy-start(f32[1,64,128]{2,1,0:T(8,128)} %weight.1) | copy-start | bytes 98308
  0.7 53.2 %copy-start.8 = (s32[64]{0:T(128)S(1)}, s32[64]{0:T(128)}, u32[]{:S(2)}) copy-start(s32[64]{0:T(128)} %param.22) | copy-start | bytes 772
  0.7 53.2 %copy-start.4 = (f32[64,128]{1,0:T(8,128)S(1)}, f32[64,128]{1,0:T(8,128)}, u32[]{:S(2)}) copy-start(f32[64,128]{1,0:T(8,128)} %momentum.1) | copy-start | bytes 98308
  0.7 53.2 %copy-start.7 = (f32[1,64]{1,0:T(1,128)S(1)}, f32[1,64]{1,0:T(1,128)}, u32[]{:S(2)}) copy-start(f32[1,64]{1,0:T(1,128)} %gain_v.1) | copy-start | bytes 772
  0.7 53.2 %copy-start.6 = (f32[1,64]{1,0:T(1,128)S(1)}, f32[1,64]{1,0:T(1,128)}, u32[]{:S(2)}) copy-start(f32[1,64]{1,0:T(1,128)} %gain_m.1) | copy-start | bytes 772
  0.7 53.2 %copy-start.3 = (f32[1,64,128]{2,1,0:T(8,128)S(1)}, f32[1,64,128]{2,1,0:T(8,128)}, u32[]{:S(2)}) copy-start(f32[1,64,128]{2,1,0:T(8,128)} %weight_v.1) | copy-start | bytes 98308
  0.7 53.2 %copy-start.2 = (f32[1,64,128]{2,1,0:T(8,128)S(1)}, f32[1,64,128]{2,1,0:T(8,128)}, u32[]{:S(2)}) copy-start(f32[1,64,128]{2,1,0:T(8,128)} %weight_m.1) | copy-start | bytes 98308
